TPU v7x, 32 devices: a whole 2x2x4 slice. The times are simulated.
32 devices in a mesh: groups: 2 (over x), lines: 16 (over z, y, core).
Axes of the slice: x: 2, y: 2, z: 4, core: 2. Of those that a mesh axis runs over, the one named last changes fastest.
Arguments:
- base_flow: bfloat16 [32768, 1024], P('lines', 'groups'), parts along dimension 1, may hold values from -6 to 6
- lodf_blocks: bfloat16 [3072, 128, 128], P('lines'), may hold values from -0.1796875 to 0.1796875
- block_row: int32 [3072], P('lines'), may hold values from 0 to 15, as said below
- block_col: int32 [3072], P('lines'), may hold values from 0 to 15, as said below
- block_count: int32 [16], P('lines'), may hold values from 64 to 192, as said below
- outage: int32 [2048], P('lines'), may hold values from 0 to 2047
- rating: int32 [32768], P('lines'), may hold values from 50 to 299
- cost: float32 [32768], P('lines'), may hold values from 0.3 to 9
Outputs:
- post_flow: bfloat16 [32768, 1024], P('lines', 'groups'), parts along dimension 1
- penalty: float32 [1024], P('groups'), parts along dimension 0
There are 2 independent parts, one for each index of `groups`. A program takes and returns all parts, laid end to end along the dimension named above; an argument that names none is the same for every part. Nothing has to cross between parts.
Inputs may be any that keep to these rules, and one draw needn't show every extreme that they name: Within one area the slots name distinct pairs of block_row and block_col, used slots and unused alike. `block_col`: the slot of area a names an area at most 6 steps from a along lines, counted with wrap around. `block_count`: slots of an area past its count are unused.
All inputs are finite; a program needn't handle non-finite values.
Results may differ from a plain program's by a relative error of at most 0.001.
Values may be sent and summed in bfloat16 or wider, within the bound.
A program may use at most 64 MiB of HBM per device.

v0:
```python
import jax
import jax.numpy as jnp
from jax import lax
from jax.sharding import PartitionSpec as P

SLOT_GROUP = 32
REACH = 6


def passed_along(array, axis, by):
    length = lax.axis_size(axis)
    return lax.ppermute(array, axis, [(i, (i + by) % length) for i in range(length)])


def on_device(base_flow, lodf_blocks, block_row, block_col, block_count, outage, rating, cost):
    areas = lax.axis_size("lines")
    here = lax.axis_index("lines")
    blk = lodf_blocks.shape[1]
    line_dev, scen = base_flow.shape
    rows_blocks = line_dev // blk
    panel = jnp.take(base_flow, outage, axis=0)
    below = []
    above = []
    for step in range(1, REACH + 1):
        below.append(passed_along(panel, "lines", step))
        above.append(passed_along(panel, "lines", -step))
    table = jnp.stack(below[::-1] + [panel] + above, axis=0)

    def fetch(cols):
        offset = (cols - here + REACH) % areas
        return jnp.take(table, offset, axis=0)

    count = block_count[0]
    row_ids = jnp.arange(rows_blocks, dtype=jnp.int32)

    def add_group(group, acc):
        start = group * SLOT_GROUP
        blocks = lax.dynamic_slice_in_dim(lodf_blocks, start, SLOT_GROUP, 0)
        rows = lax.dynamic_slice_in_dim(block_row, start, SLOT_GROUP, 0)
        cols = lax.dynamic_slice_in_dim(block_col, start, SLOT_GROUP, 0)
        pieces = fetch(cols)
        terms = jnp.einsum("gij,gjs->gis", blocks, pieces, preferred_element_type=jnp.float32)
        used = (start + jnp.arange(SLOT_GROUP, dtype=jnp.int32) < count).astype(jnp.float32)
        picker = (rows[None, :] == row_ids[:, None]).astype(jnp.float32) * used[None, :]
        return acc + jnp.einsum("rg,gis->ris", picker, terms, precision=lax.Precision.HIGHEST)

    groups_used = (count + SLOT_GROUP - 1) // SLOT_GROUP
    added = lax.fori_loop(
        0, groups_used, add_group, jnp.zeros((rows_blocks, blk, scen), jnp.float32)
    )
    post = base_flow.astype(jnp.float32) + added.reshape(line_dev, scen)
    limit = 0.01 * rating.astype(jnp.float32)
    excess = jnp.maximum(jnp.abs(post) - limit[:, None], 0.0)
    share = jnp.sum(cost[:, None] * excess * excess, axis=0)
    total = lax.psum(share, "lines")
    return (post.astype(jnp.bfloat16), total / (line_dev * areas))


def solution(mesh):
    return jax.shard_map(
        on_device,
        mesh=mesh,
        in_specs=(
            P("lines", "groups"),
            P("lines", None, None),
            P("lines"),
            P("lines"),
            P("lines"),
            P("lines"),
            P("lines"),
            P("lines"),
        ),
        out_specs=(P("lines", "groups"), P("groups")),
        check_vma=False,
    )
```

profile of v0, /device:TPU:0, one launch (start us, length us, event | category | flops | bytes accessed | tf_op | source)
XLA Modules:
  0.0 202.0 jit_solution(4122475913397345986)
XLA Ops:
  0.6 0.7 compare_select_fusion.3
  1.3 0.7 compare_and_fusion.1
  2.0 2.7 %gather_fusion.1 = bf16[128,512]{1,0:T(8,128)(2,1)S(1)} fusion(bf16[2048,512]{1,0:T(8,128)(2,1)} %param.10, s32[1024]{0:T(1024)S(1)} %pad_clamp_fusion.1), kind=kCustom, calls=%fused_computation.1 | custom fusion | bytes 262656 | tf_op jit(solution)/shard_map/jit(_take)/gather | solution.py:21
  4.8 4.0 %collective-permute-start = (bf16[128,512]{1,0:T(8,128)(2,1)S(1)}, bf16[128,512]{1,0:T(8,128)(2,1)S(1)}, u32[]{:S(2)}, u32[]{:S(2)}) collective-permute-start(bf16[128,512]{1,0:T(8,128)(2,1)S(1)} %broadcast_select_fusion), channel_id=1, source_target_pairs={{0,6},{1,7},{2,8},{3,9},{4,10},{5,11},{6,12},{7,13},{8,14},{9,15},... | collective-permute-start | bytes 393224 | tf_op jit(solution)/shard_map/ppermute | solution.py:12
  8.8 0.7 collective-permute-start.1
  9.6 1.6 collective-permute-start.2
  11.1 1.5 collective-permute-start.3
  12.6 0.6 collective-permute-start.4
  13.8 0.7 convert_multiply_fusion
  14.5 13.7 %collective-permute-done = bf16[128,512]{1,0:T(8,128)(2,1)S(1)} collective-permute-done((bf16[128,512]{1,0:T(8,128)(2,1)S(1)}, bf16[128,512]{1,0:T(8,128)(2,1)S(1)}, u32[]{:S(2)}, u32[]{:S(2)}) %collective-permute-start) | collective-permute-done | bytes 131104 | tf_op jit(solution)/shard_map/ppermute | solution.py:12
  28.8 3.9 %collective-permute-start.6 = (bf16[128,512]{1,0:T(8,128)(2,1)S(1)}, bf16[128,512]{1,0:T(8,128)(2,1)S(1)}, u32[]{:S(2)}, u32[]{:S(2)}) collective-permute-start(bf16[128,512]{1,0:T(8,128)(2,1)S(1)} %broadcast_select_fusion), channel_id=1, source_target_pairs={{0,15},{1,0},{2,1},{3,2},{4,3},{5,4},{6,5},{7,6},{8,7},{9,8},{10,9... | collective-permute-start | bytes 393224 | tf_op jit(solution)/shard_map/ppermute | solution.py:12
  33.0 3.7 %collective-permute-done.5 = bf16[128,512]{1,0:T(8,128)(2,1)S(1)} collective-permute-done((bf16[128,512]{1,0:T(8,128)(2,1)S(1)}, bf16[128,512]{1,0:T(8,128)(2,1)S(1)}, u32[]{:S(2)}, u32[]{:S(2)}) %collective-permute-start.5) | collective-permute-done | bytes 131104 | tf_op jit(solution)/shard_map/ppermute | solution.py:12
  36.9 1.9 collective-permute-start.11
  38.8 0.6 collective-permute-done.7
  39.4 2.8 %collective-permute-done.8 = bf16[128,512]{1,0:T(8,128)(2,1)S(1)} collective-permute-done((bf16[128,512]{1,0:T(8,128)(2,1)S(1)}, bf16[128,512]{1,0:T(8,128)(2,1)S(1)}, u32[]{:S(2)}, u32[]{:S(2)}) %collective-permute-start.8) | collective-permute-done | bytes 131104 | tf_op jit(solution)/shard_map/ppermute | solution.py:12
  42.2 2.8 %collective-permute-done.9 = bf16[128,512]{1,0:T(8,128)(2,1)S(1)} collective-permute-done((bf16[128,512]{1,0:T(8,128)(2,1)S(1)}, bf16[128,512]{1,0:T(8,128)(2,1)S(1)}, u32[]{:S(2)}, u32[]{:S(2)}) %collective-permute-start.9) | collective-permute-done | bytes 131104 | tf_op jit(solution)/shard_map/ppermute | solution.py:12
  45.0 2.4 %collective-permute-done.10 = bf16[128,512]{1,0:T(8,128)(2,1)S(1)} collective-permute-done((bf16[128,512]{1,0:T(8,128)(2,1)S(1)}, bf16[128,512]{1,0:T(8,128)(2,1)S(1)}, u32[]{:S(2)}, u32[]{:S(2)}) %collective-permute-start.10) | collective-permute-done | bytes 131104 | tf_op jit(solution)/shard_map/ppermute | solution.py:12
  47.4 1.4 collective-permute-done.11
  48.9 2.5 %broadcast_in_dim.45 = f32[16,128,512]{2,0,1:T(8,128)} broadcast(f32[]{:T(128)} %constant.110.clone.1), dimensions={} | broadcast | bytes 4194308 | tf_op jit(solution)/shard_map/broadcast_in_dim | solution.py:49
  51.3 108.7 %while.13 = (s32[]{:T(128)}, f32[16,128,512]{2,0,1:T(8,128)}, s32[]{:T(128)}, s32[192]{0:T(256)S(1)}, s32[]{:T(128)}, /*index=5*/bf16[192,128,128]{2,1,0:T(8,128...) while((s32[]{:T(128)}, f32[16,128,512]{2,0,1:T(8,128)}, ...), condition=%wide.region_1.2_spmd.clone, body=%wide.region_0.1_spmd.clone.sunk | while | flops 942672576 | bytes 38802816 | solution.py:48
  51.3 0.7 compare_and_fusion.3
  52.1 2.8 %gather_fusion = bf16[32,128,512]{2,1,0:T(8,128)(2,1)} fusion(bf16[13,128,512]{2,1,0:T(8,128)(2,1)S(1)} %get-tuple-element.272, s32[1024]{0:T(1024)S(1)} %pad_clamp_fusion.3), kind=kCustom, calls=%fused_computation.clone.clone.1 | custom fusion | bytes 8388736 | tf_op jit(solution)/shard_map/while/body/jit(_take)/gather | solution.py:31
  54.9 3.8 %fusion.34 = f32[32,128,512]{2,1,0:T(8,128)S(1)} fusion(bf16[32,128,512]{2,1,0:T(8,128)(2,1)} %gather_fusion, pred[32]{0:T(512)(128)(4,1)S(1)} %get-tuple-element.236, bf16[192,128,128]{2,1,0:T(8,128)(2,1)} %get-tuple-element.269, s32[]{:T(128)S(6)} %select_n.84), kind=kOutput, calls=%fused_computation.5.clone.1 | convolution fusion | flops 538968064 | bytes 13631524 | tf_op jit(solution)/shard_map/while/body/gij,gjs->gis/dot_general | solution.py:42
  58.8 10.7 %fusion.35 = f32[16,128,512]{2,0,1:T(8,128)} fusion(f32[16,128,512]{2,0,1:T(8,128)} %get-tuple-element.252, f32[32,128,512]{2,1,0:T(8,128)S(1)} %fusion.34, f32[32]{0:T(128)S(1)} %get-tuple-element.237, s32[32]{0:T(128)S(1)} %dynamic_slice.28), kind=kOutput, calls=%fused_computation.8.clone.1 | convolution fusion | flops 403702784 | bytes 16777472 | tf_op jit(solution)/shard_map/while/body/rg,gis->ris/dot_general | solution.py:45
  69.5 0.7 compare_and_fusion.3
  70.2 2.8 %gather_fusion = bf16[32,128,512]{2,1,0:T(8,128)(2,1)} fusion(bf16[13,128,512]{2,1,0:T(8,128)(2,1)S(1)} %get-tuple-element.272, s32[1024]{0:T(1024)S(1)} %pad_clamp_fusion.3), kind=kCustom, calls=%fused_computation.clone.clone.1 | custom fusion | bytes 8388736 | tf_op jit(solution)/shard_map/while/body/jit(_take)/gather | solution.py:31
  73.0 3.8 %fusion.34 = f32[32,128,512]{2,1,0:T(8,128)S(1)} fusion(bf16[32,128,512]{2,1,0:T(8,128)(2,1)} %gather_fusion, pred[32]{0:T(512)(128)(4,1)S(1)} %get-tuple-element.236, bf16[192,128,128]{2,1,0:T(8,128)(2,1)} %get-tuple-element.269, s32[]{:T(128)S(6)} %select_n.84), kind=kOutput, calls=%fused_computation.5.clone.1 | convolution fusion | flops 538968064 | bytes 13631524 | tf_op jit(solution)/shard_map/while/body/gij,gjs->gis/dot_general | solution.py:42
  76.9 10.7 %fusion.35 = f32[16,128,512]{2,0,1:T(8,128)} fusion(f32[16,128,512]{2,0,1:T(8,128)} %get-tuple-element.252, f32[32,128,512]{2,1,0:T(8,128)S(1)} %fusion.34, f32[32]{0:T(128)S(1)} %get-tuple-element.237, s32[32]{0:T(128)S(1)} %dynamic_slice.28), kind=kOutput, calls=%fused_computation.8.clone.1 | convolution fusion | flops 403702784 | bytes 16777472 | tf_op jit(solution)/shard_map/while/body/rg,gis->ris/dot_general | solution.py:45
  87.6 0.7 compare_and_fusion.3
  88.3 2.8 %gather_fusion = bf16[32,128,512]{2,1,0:T(8,128)(2,1)} fusion(bf16[13,128,512]{2,1,0:T(8,128)(2,1)S(1)} %get-tuple-element.272, s32[1024]{0:T(1024)S(1)} %pad_clamp_fusion.3), kind=kCustom, calls=%fused_computation.clone.clone.1 | custom fusion | bytes 8388736 | tf_op jit(solution)/shard_map/while/body/jit(_take)/gather | solution.py:31
  91.1 3.8 %fusion.34 = f32[32,128,512]{2,1,0:T(8,128)S(1)} fusion(bf16[32,128,512]{2,1,0:T(8,128)(2,1)} %gather_fusion, pred[32]{0:T(512)(128)(4,1)S(1)} %get-tuple-element.236, bf16[192,128,128]{2,1,0:T(8,128)(2,1)} %get-tuple-element.269, s32[]{:T(128)S(6)} %select_n.84), kind=kOutput, calls=%fused_computation.5.clone.1 | convolution fusion | flops 538968064 | bytes 13631524 | tf_op jit(solution)/shard_map/while/body/gij,gjs->gis/dot_general | solution.py:42
  95.0 10.7 %fusion.35 = f32[16,128,512]{2,0,1:T(8,128)} fusion(f32[16,128,512]{2,0,1:T(8,128)} %get-tuple-element.252, f32[32,128,512]{2,1,0:T(8,128)S(1)} %fusion.34, f32[32]{0:T(128)S(1)} %get-tuple-element.237, s32[32]{0:T(128)S(1)} %dynamic_slice.28), kind=kOutput, calls=%fused_computation.8.clone.1 | convolution fusion | flops 403702784 | bytes 16777472 | tf_op jit(solution)/shard_map/while/body/rg,gis->ris/dot_general | solution.py:45
  105.7 0.7 compare_and_fusion.3
  106.5 2.8 %gather_fusion = bf16[32,128,512]{2,1,0:T(8,128)(2,1)} fusion(bf16[13,128,512]{2,1,0:T(8,128)(2,1)S(1)} %get-tuple-element.272, s32[1024]{0:T(1024)S(1)} %pad_clamp_fusion.3), kind=kCustom, calls=%fused_computation.clone.clone.1 | custom fusion | bytes 8388736 | tf_op jit(solution)/shard_map/while/body/jit(_take)/gather | solution.py:31
  109.3 3.8 %fusion.34 = f32[32,128,512]{2,1,0:T(8,128)S(1)} fusion(bf16[32,128,512]{2,1,0:T(8,128)(2,1)} %gather_fusion, pred[32]{0:T(512)(128)(4,1)S(1)} %get-tuple-element.236, bf16[192,128,128]{2,1,0:T(8,128)(2,1)} %get-tuple-element.269, s32[]{:T(128)S(6)} %select_n.84), kind=kOutput, calls=%fused_computation.5.clone.1 | convolution fusion | flops 538968064 | bytes 13631524 | tf_op jit(solution)/shard_map/while/body/gij,gjs->gis/dot_general | solution.py:42
  113.2 10.7 %fusion.35 = f32[16,128,512]{2,0,1:T(8,128)} fusion(f32[16,128,512]{2,0,1:T(8,128)} %get-tuple-element.252, f32[32,128,512]{2,1,0:T(8,128)S(1)} %fusion.34, f32[32]{0:T(128)S(1)} %get-tuple-element.237, s32[32]{0:T(128)S(1)} %dynamic_slice.28), kind=kOutput, calls=%fused_computation.8.clone.1 | convolution fusion | flops 403702784 | bytes 16777472 | tf_op jit(solution)/shard_map/while/body/rg,gis->ris/dot_general | solution.py:45
  123.8 0.7 compare_and_fusion.3
  124.6 2.8 %gather_fusion = bf16[32,128,512]{2,1,0:T(8,128)(2,1)} fusion(bf16[13,128,512]{2,1,0:T(8,128)(2,1)S(1)} %get-tuple-element.272, s32[1024]{0:T(1024)S(1)} %pad_clamp_fusion.3), kind=kCustom, calls=%fused_computation.clone.clone.1 | custom fusion | bytes 8388736 | tf_op jit(solution)/shard_map/while/body/jit(_take)/gather | solution.py:31
  127.4 3.8 %fusion.34 = f32[32,128,512]{2,1,0:T(8,128)S(1)} fusion(bf16[32,128,512]{2,1,0:T(8,128)(2,1)} %gather_fusion, pred[32]{0:T(512)(128)(4,1)S(1)} %get-tuple-element.236, bf16[192,128,128]{2,1,0:T(8,128)(2,1)} %get-tuple-element.269, s32[]{:T(128)S(6)} %select_n.84), kind=kOutput, calls=%fused_computation.5.clone.1 | convolution fusion | flops 538968064 | bytes 13631524 | tf_op jit(solution)/shard_map/while/body/gij,gjs->gis/dot_general | solution.py:42
  131.3 10.7 %fusion.35 = f32[16,128,512]{2,0,1:T(8,128)} fusion(f32[16,128,512]{2,0,1:T(8,128)} %get-tuple-element.252, f32[32,128,512]{2,1,0:T(8,128)S(1)} %fusion.34, f32[32]{0:T(128)S(1)} %get-tuple-element.237, s32[32]{0:T(128)S(1)} %dynamic_slice.28), kind=kOutput, calls=%fused_computation.8.clone.1 | convolution fusion | flops 403702784 | bytes 16777472 | tf_op jit(solution)/shard_map/while/body/rg,gis->ris/dot_general | solution.py:45
  142.0 0.7 compare_and_fusion.3
  142.7 2.8 %gather_fusion = bf16[32,128,512]{2,1,0:T(8,128)(2,1)} fusion(bf16[13,128,512]{2,1,0:T(8,128)(2,1)S(1)} %get-tuple-element.272, s32[1024]{0:T(1024)S(1)} %pad_clamp_fusion.3), kind=kCustom, calls=%fused_computation.clone.clone.1 | custom fusion | bytes 8388736 | tf_op jit(solution)/shard_map/while/body/jit(_take)/gather | solution.py:31
  145.5 3.8 %fusion.34 = f32[32,128,512]{2,1,0:T(8,128)S(1)} fusion(bf16[32,128,512]{2,1,0:T(8,128)(2,1)} %gather_fusion, pred[32]{0:T(512)(128)(4,1)S(1)} %get-tuple-element.236, bf16[192,128,128]{2,1,0:T(8,128)(2,1)} %get-tuple-element.269, s32[]{:T(128)S(6)} %select_n.84), kind=kOutput, calls=%fused_computation.5.clone.1 | convolution fusion | flops 538968064 | bytes 13631524 | tf_op jit(solution)/shard_map/while/body/gij,gjs->gis/dot_general | solution.py:42
  149.4 10.7 %fusion.35 = f32[16,128,512]{2,0,1:T(8,128)} fusion(f32[16,128,512]{2,0,1:T(8,128)} %get-tuple-element.252, f32[32,128,512]{2,1,0:T(8,128)S(1)} %fusion.34, f32[32]{0:T(128)S(1)} %get-tuple-element.237, s32[32]{0:T(128)S(1)} %dynamic_slice.28), kind=kOutput, calls=%fused_computation.8.clone.1 | convolution fusion | flops 403702784 | bytes 16777472 | tf_op jit(solution)/shard_map/while/body/rg,gis->ris/dot_general | solution.py:45
  160.1 4.8 %copy.10 = f32[16,128,512]{2,1,0:T(8,128)S(1)} copy(f32[16,128,512]{2,0,1:T(8,128)} %get-tuple-element.131) | data formatting | bytes 8388608 | tf_op jit(solution)/shard_map/while | solution.py:48
  164.9 2.5 %fusion.21 = (f32[512]{0:T(512)S(1)}, bf16[2048,512]{1,0:T(8,128)(2,1)}) fusion(f32[16,128,512]{2,1,0:T(8,128)S(1)} %copy.10, bf16[2048,512]{1,0:T(8,128)(2,1)S(1)} %copy-done, f32[2048]{0:T(1024)S(1)} %convert_multiply_fusion, f32[2048]{0:T(1024)S(1)} %copy-done.1), kind=kLoop, calls=%fused_computation.29 | loop fusion | flops 9436672 | bytes 8407040 | tf_op jit(solution)/shard_map/reduce_sum | solution.py:54
  167.4 34.0 %psum.7 = f32[512]{0:T(512)S(1)} all-reduce(f32[512]{0:T(512)S(1)} %get-tuple-element.174), channel_id=1, replica_groups=mesh['groups'=2,'lines'=16] {'lines'}, use_global_device_ids=true, to_apply=%region_3.4 | all-reduce | flops 512 | bytes 4096 | tf_op jit(solution)/shard_map/psum | solution.py:55
  201.4 0.6 broadcast_multiply_fusion
  (45 shorter events, 1.6 us)
Async XLA Ops:
  4.8 23.4 %collective-permute-start = (bf16[128,512]{1,0:T(8,128)(2,1)S(1)}, bf16[128,512]{1,0:T(8,128)(2,1)S(1)}, u32[]{:S(2)}, u32[]{:S(2)}) collective-permute-start(bf16[128,512]{1,0:T(8,128)(2,1)S(1)} %broadcast_select_fusion), channel_id=1, source_target_pairs={{0,6},{1,7},{2,8},{3,9},{4,10},{5,11},{6,12},{7,13},{8,14},{9,15},... | collective-permute-start | bytes 393224 | tf_op jit(solution)/shard_map/ppermute | solution.py:12
  8.8 20.0 %collective-permute-start.1 = (bf16[128,512]{1,0:T(8,128)(2,1)S(1)}, bf16[128,512]{1,0:T(8,128)(2,1)S(1)}, u32[]{:S(2)}, u32[]{:S(2)}) collective-permute-start(bf16[128,512]{1,0:T(8,128)(2,1)S(1)} %broadcast_select_fusion), channel_id=1, source_target_pairs={{0,5},{1,6},{2,7},{3,8},{4,9},{5,10},{6,11},{7,12},{8,13},{9,14},{... | collective-permute-start | bytes 393224 | tf_op jit(solution)/shard_map/ppermute | solution.py:12
  9.6 23.2 %collective-permute-start.2 = (bf16[128,512]{1,0:T(8,128)(2,1)S(1)}, bf16[128,512]{1,0:T(8,128)(2,1)S(1)}, u32[]{:S(2)}, u32[]{:S(2)}) collective-permute-start(bf16[128,512]{1,0:T(8,128)(2,1)S(1)} %broadcast_select_fusion), channel_id=1, source_target_pairs={{0,4},{1,5},{2,6},{3,7},{4,8},{5,9},{6,10},{7,11},{8,12},{9,13},{1... | collective-permute-start | bytes 393224 | tf_op jit(solution)/shard_map/ppermute | solution.py:12
  11.1 21.7 %collective-permute-start.3 = (bf16[128,512]{1,0:T(8,128)(2,1)S(1)}, bf16[128,512]{1,0:T(8,128)(2,1)S(1)}, u32[]{:S(2)}, u32[]{:S(2)}) collective-permute-start(bf16[128,512]{1,0:T(8,128)(2,1)S(1)} %broadcast_select_fusion), channel_id=1, source_target_pairs={{0,3},{1,4},{2,5},{3,6},{4,7},{5,8},{6,9},{7,10},{8,11},{9,12},{10... | collective-permute-start | bytes 393224 | tf_op jit(solution)/shard_map/ppermute | solution.py:12
  12.6 20.3 %collective-permute-start.4 = (bf16[128,512]{1,0:T(8,128)(2,1)S(1)}, bf16[128,512]{1,0:T(8,128)(2,1)S(1)}, u32[]{:S(2)}, u32[]{:S(2)}) collective-permute-start(bf16[128,512]{1,0:T(8,128)(2,1)S(1)} %broadcast_select_fusion), channel_id=1, source_target_pairs={{0,2},{1,3},{2,4},{3,5},{4,6},{5,7},{6,8},{7,9},{8,10},{9,11},{10,... | collective-permute-start | bytes 393224 | tf_op jit(solution)/shard_map/ppermute | solution.py:12
  28.2 8.5 %collective-permute-start.5 = (bf16[128,512]{1,0:T(8,128)(2,1)S(1)}, bf16[128,512]{1,0:T(8,128)(2,1)S(1)}, u32[]{:S(2)}, u32[]{:S(2)}) collective-permute-start(bf16[128,512]{1,0:T(8,128)(2,1)S(1)} %broadcast_select_fusion), channel_id=1, source_target_pairs={{0,1},{1,2},{2,3},{3,4},{4,5},{5,6},{6,7},{7,8},{8,9},{9,10},{10,1... | collective-permute-start | bytes 393224 | tf_op jit(solution)/shard_map/ppermute | solution.py:12
  28.8 8.1 %collective-permute-start.6 = (bf16[128,512]{1,0:T(8,128)(2,1)S(1)}, bf16[128,512]{1,0:T(8,128)(2,1)S(1)}, u32[]{:S(2)}, u32[]{:S(2)}) collective-permute-start(bf16[128,512]{1,0:T(8,128)(2,1)S(1)} %broadcast_select_fusion), channel_id=1, source_target_pairs={{0,15},{1,0},{2,1},{3,2},{4,3},{5,4},{6,5},{7,6},{8,7},{9,8},{10,9... | collective-permute-start | bytes 393224 | tf_op jit(solution)/shard_map/ppermute | solution.py:12
  32.8 6.6 %collective-permute-start.7 = (bf16[128,512]{1,0:T(8,128)(2,1)S(1)}, bf16[128,512]{1,0:T(8,128)(2,1)S(1)}, u32[]{:S(2)}, u32[]{:S(2)}) collective-permute-start(bf16[128,512]{1,0:T(8,128)(2,1)S(1)} %broadcast_select_fusion), channel_id=1, source_target_pairs={{0,14},{1,15},{2,0},{3,1},{4,2},{5,3},{6,4},{7,5},{8,6},{9,7},{10,... | collective-permute-start | bytes 393224 | tf_op jit(solution)/shard_map/ppermute | solution.py:12
  32.8 9.4 %collective-permute-start.8 = (bf16[128,512]{1,0:T(8,128)(2,1)S(1)}, bf16[128,512]{1,0:T(8,128)(2,1)S(1)}, u32[]{:S(2)}, u32[]{:S(2)}) collective-permute-start(bf16[128,512]{1,0:T(8,128)(2,1)S(1)} %broadcast_select_fusion), channel_id=1, source_target_pairs={{0,13},{1,14},{2,15},{3,0},{4,1},{5,2},{6,3},{7,4},{8,5},{9,6},{10... | collective-permute-start | bytes 393224 | tf_op jit(solution)/shard_map/ppermute | solution.py:12
  32.9 12.1 %collective-permute-start.9 = (bf16[128,512]{1,0:T(8,128)(2,1)S(1)}, bf16[128,512]{1,0:T(8,128)(2,1)S(1)}, u32[]{:S(2)}, u32[]{:S(2)}) collective-permute-start(bf16[128,512]{1,0:T(8,128)(2,1)S(1)} %broadcast_select_fusion), channel_id=1, source_target_pairs={{0,12},{1,13},{2,14},{3,15},{4,0},{5,1},{6,2},{7,3},{8,4},{9,5},{1... | collective-permute-start | bytes 393224 | tf_op jit(solution)/shard_map/ppermute | solution.py:12
  36.7 10.7 %collective-permute-start.10 = (bf16[128,512]{1,0:T(8,128)(2,1)S(1)}, bf16[128,512]{1,0:T(8,128)(2,1)S(1)}, u32[]{:S(2)}, u32[]{:S(2)}) collective-permute-start(bf16[128,512]{1,0:T(8,128)(2,1)S(1)} %broadcast_select_fusion), channel_id=1, source_target_pairs={{0,11},{1,12},{2,13},{3,14},{4,15},{5,0},{6,1},{7,2},{8,3},{9,4},{... | collective-permute-start | bytes 393224 | tf_op jit(solution)/shard_map/ppermute | solution.py:12
  36.9 12.0 %collective-permute-start.11 = (bf16[128,512]{1,0:T(8,128)(2,1)S(1)}, bf16[128,512]{1,0:T(8,128)(2,1)S(1)}, u32[]{:S(2)}, u32[]{:S(2)}) collective-permute-start(bf16[128,512]{1,0:T(8,128)(2,1)S(1)} %broadcast_select_fusion), channel_id=1, source_target_pairs={{0,10},{1,11},{2,12},{3,13},{4,14},{5,15},{6,0},{7,1},{8,2},{9,3},... | collective-permute-start | bytes 393224 | tf_op jit(solution)/shard_map/ppermute | solution.py:12
  48.8 2.5 %copy-start.2 = (s32[192]{0:T(256)S(1)}, s32[192]{0:T(256)}, u32[]{:S(2)}) copy-start(s32[192]{0:T(256)} %param.13) | copy-start | bytes 2308
  48.8 2.5 %copy-start.3 = (s32[192]{0:T(256)S(1)}, s32[192]{0:T(256)}, u32[]{:S(2)}) copy-start(s32[192]{0:T(256)} %param.12) | copy-start | bytes 2308
  160.1 4.8 %copy-start = (bf16[2048,512]{1,0:T(8,128)(2,1)S(1)}, bf16[2048,512]{1,0:T(8,128)(2,1)}, u32[]{:S(2)}) copy-start(bf16[2048,512]{1,0:T(8,128)(2,1)} %param.10) | copy-start | bytes 6291460
  160.1 4.8 %copy-start.1 = (f32[2048]{0:T(1024)S(1)}, f32[2048]{0:T(1024)}, u32[]{:S(2)}) copy-start(f32[2048]{0:T(1024)} %param.17) | copy-start | bytes 24580
where the time goes:
time: 202 us
  matrix products  87 us (43%)
  blocking collectives  34 us (17%)
  waiting for transfers between devices  27.9 us (14%)
  local copies, waits for them, and re-layouts  27.3 us (14%)
  starting transfers between devices  14.4 us (7%)
  other arithmetic  9.72 us (5%)
    dot_general x6, matrix products, add_group(): jnp.einsum('rg,gis->ris', picker, terms, precision=lax.Precision.HIGHEST)  64.1 us
    psum x1, blocking collectives, on_device(): total = lax.psum(share, 'lines')  34 us
    ppermute x12, waiting for transfers between devices, passed_along(): lax.ppermute(array, axis, [(i, (i + by) % length) for i in range(length)])  27.9 us
    dot_general x6, matrix products, add_group(): jnp.einsum('gij,gjs->gis', blocks, pieces, preferred_element_type=jnp.flo...  22.9 us
    gather x6, local copies, waits for them, and re-layouts, fetch(): return jnp.take(table, offset, axis=0)  16.7 us
    ppermute x12, starting transfers between devices, passed_along(): lax.ppermute(array, axis, [(i, (i + by) % length) for i in range(length)])  14.4 us
    while x1, local copies, waits for them, and re-layouts, on_device(): lax.fori_loop(0, groups_used, add_group, jnp.zeros((rows_blocks, blk, sce...  4.77 us
    and x6, other arithmetic, fetch(): return jnp.take(table, offset, axis=0)  4.4 us
  transfers between devices with their start and end apart: 12, of which 8 were waited for; matrix products, arithmetic and copies ran while one was open for 0% of the time, Pallas kernels for 0%

commit v1 on v0

v1 whole, which is shorter than its diff:
```python
import functools

import jax
import jax.numpy as jnp
from jax import lax
from jax.experimental import pallas as pl
from jax.experimental.pallas import tpu as pltpu
from jax.sharding import PartitionSpec as P

REACH = 6
NEAR = REACH // 2
MESH = pl.DeviceIdType.MESH
ROWS = 512
LAST_ROWS = 256


def kernel(areas, base_hbm, lodf_hbm, row_ref, col_ref, count_ref, outage_ref, rating_ref, cost_ref,
           post_hbm, pen_ref, base, lodf, table, inv_v, inv_s, panels, acc, post, limit, weight,
           shares, in_sem, out_sem, inv_sem, z_send, y_send, core_send, off_recv, core_recv,
           pen_send, pen_recv):
    chips = areas // 2
    small = chips == 8
    line_dev, scen = base.shape
    blk = lodf.shape[1]
    nb = lodf.shape[0] - 1
    rows_blocks = line_dev // blk
    width = 2 * (2 * NEAR + 1)
    here = lax.axis_index("lines")
    core = lax.rem(here, 2)
    chip = here // 2
    partner = chip * 2 + 1 - core

    base_in = pltpu.make_async_copy(base_hbm, base, in_sem.at[0])
    base_in.start()
    lodf_in = pltpu.make_async_copy(lodf_hbm, lodf.at[pl.ds(0, nb)], in_sem.at[1])
    lodf_in.start()

    barrier = pltpu.get_barrier_semaphore()
    if small:
        peers = [lax.rem(here + step, areas) for step in range(1, areas)]
    else:
        peers = [lax.rem(here + 2 * step + areas, areas) for step in range(-NEAR, NEAR + 1) if step != 0]
        peers.append(partner)
    for peer in peers:
        pl.semaphore_signal(barrier, inc=1, device_id={"lines": peer}, device_id_type=MESH)

    def slot(of, at):
        return lax.rem(of - at + NEAR + chips, chips)

    def remote(of, to_chip, to_core, send_sem, recv_sem):
        there = slot(of, to_chip)
        return pltpu.make_async_remote_copy(
            src_ref=panels.at[slot(of, chip), core],
            dst_ref=panels.at[there, core],
            send_sem=send_sem,
            recv_sem=recv_sem.at[there],
            device_id={"lines": to_chip * 2 + to_core},
            device_id_type=MESH,
        )

    def to_core(of):
        return remote(of, chip, 1 - core, core_send.at[slot(of, chip)], core_recv)

    def off_wait(of):
        remote(of, chip, core, y_send.at[0], off_recv).wait_recv()

    picked = jnp.transpose(jnp.broadcast_to(outage_ref[...].astype(jnp.float32), (blk, blk)))
    lane = lax.broadcasted_iota(jnp.int32, (blk, blk), 1)
    ones = jnp.concatenate(
        [(picked == (lane + part * blk).astype(jnp.float32)).astype(jnp.bfloat16) for part in range(rows_blocks)],
        axis=1,
    )
    base_in.wait()
    panels[NEAR, core] = jnp.dot(ones, base[...], preferred_element_type=jnp.float32).astype(jnp.bfloat16)
    pl.semaphore_wait(barrier, len(peers))

    to_core(chip).start()
    if small:
        y = lax.rem(chip, 2)
        z = chip // 2
        across = chip + 1 - 2 * y
        first, last, high = (3 - z) // 3, z // 3, z // 2
        steps = [0, 1 - 2 * last, 3 * first - 1 - last, 2 - 4 * high + first - last]
        signs = [0, 1 - 2 * last, 2 * first - 1, 1 - 2 * high]

        def to_y(of):
            return remote(of, across, core, y_send.at[slot(of, chip)], off_recv)

        def to_z(of, by):
            return remote(of, chip + 2 * by, core, z_send.at[slot(of, chip), (by + 1) // 2], off_recv)

        to_y(chip).start()
        up, down = to_z(chip, 1), to_z(chip, -1)

        @pl.when(z < 3)
        def _():
            up.start()

        @pl.when(z > 0)
        def _():
            down.start()
    else:
        away = [step for step in range(-NEAR, NEAR + 1) if step != 0]

        def direct(step):
            to_chip = lax.rem(chip + step + chips, chips)
            return remote(chip, to_chip, core, y_send.at[step + NEAR], off_recv)

        for step in away:
            direct(step).start()

    offset = lax.rem(col_ref[...] - (2 * chip - REACH) + 2 * areas, areas)
    number = lax.broadcasted_iota(jnp.int32, (1, nb), 1)
    code = jnp.where(number < count_ref[0], row_ref[...] * width + offset, -1)
    pair = lax.broadcasted_iota(jnp.int32, (rows_blocks * width, nb), 0)
    found = jnp.sum(jnp.where(pair == code, number - nb, 0), axis=1, keepdims=True) + nb
    inv_v[...] = jnp.broadcast_to(found, inv_v.shape)
    inv_copy = pltpu.make_async_copy(inv_v, inv_s, inv_sem)
    inv_copy.start()
    lodf[nb] = jnp.zeros((blk, blk), jnp.bfloat16)
    lodf_in.wait()
    inv_copy.wait()

    @pl.loop(0, rows_blocks)
    def _(r):
        for k in range(width):
            at = pl.ds(pl.multiple_of(r * blk, blk), blk)
            table[k // 2, at, (k % 2) * blk:(k % 2 + 1) * blk] = lodf[inv_s[r * width + k, 0]]

    def add(of, start=False):
        m = slot(of, chip)

        @pl.loop(0, line_dev // ROWS)
        def _(i):
            at = pl.ds(pl.multiple_of(i * ROWS, ROWS), ROWS)
            term = jnp.dot(
                table[m, at, :], panels[m].reshape(2 * blk, scen), preferred_element_type=jnp.float32
            )
            acc[at, :] = term if start else acc[at, :] + term

    def core_wait(of):
        to_core(of).wait_recv()

    def spread():
        for r in range(rows_blocks):
            at = slice(r * blk, (r + 1) * blk)
            bound = 0.01 * rating_ref[r:r + 1, :].astype(jnp.float32)
            limit[at, :] = jnp.transpose(jnp.broadcast_to(bound, (blk, blk)))
            weight[at, :] = jnp.transpose(jnp.broadcast_to(cost_ref[r:r + 1, :], (blk, blk)))

    if small:
        def z_event(i):
            of = chip + 2 * steps[i]
            off_wait(of)
            back = z - signs[i]

            @pl.when((back >= 0) & (back <= 3))
            def _():
                to_z(of, -signs[i]).start()

            to_y(of).start()

            @pl.when(steps[i] * signs[i] != 2)
            def _():
                to_core(of).start()

        def y_event(i):
            of = across + 2 * steps[i]
            off_wait(of)
            to_core(of).start()

        def add_z(i):
            @pl.when(steps[i] * signs[i] != 2)
            def _():
                core_wait(chip + 2 * steps[i])
                add(chip + 2 * steps[i])

        def add_y(i):
            core_wait(across + 2 * steps[i])
            add(across + 2 * steps[i])

        core_wait(chip)
        add(chip, True)
        z_event(1)
        y_event(0)
        spread()
        add_y(0)
        z_event(2)
        y_event(1)
        add_z(1)
        add_y(1)
        z_event(3)
        y_event(2)
        add_z(2)
        add_y(2)
        add_z(3)
        y_event(3)
        final = across + 2 * steps[3]
        core_wait(final)
    else:
        core_wait(chip)
        add(chip, True)
        spread()
        near = [1, -1, 2, -2, 3, -3]
        for step in near:
            of = lax.rem(chip + step + chips, chips)
            off_wait(of)
            to_core(of).start()
        for step in near[:-1]:
            of = lax.rem(chip + step + chips, chips)
            core_wait(of)
            add(of)
        final = lax.rem(chip + near[-1] + chips, chips)
        core_wait(final)

    m = slot(final, chip)

    def post_out(i):
        at = pl.ds(pl.multiple_of(i * LAST_ROWS, LAST_ROWS), LAST_ROWS)
        return pltpu.make_async_copy(post.at[at], post_hbm.at[at], out_sem.at[i])

    def last_pass(i, share):
        at = pl.ds(pl.multiple_of(i * LAST_ROWS, LAST_ROWS), LAST_ROWS)
        term = jnp.dot(table[m, at, :], panels[m].reshape(2 * blk, scen), preferred_element_type=jnp.float32)
        flow = base[at, :].astype(jnp.float32) + (acc[at, :] + term)
        post[at, :] = flow.astype(jnp.bfloat16)
        post_out(i).start()
        bound = jnp.concatenate([limit[at, :]] * (scen // blk), axis=1)
        each = jnp.concatenate([weight[at, :]] * (scen // blk), axis=1)
        excess = jnp.maximum(jnp.abs(flow) - bound, 0.0)
        return share + jnp.sum((each * excess * excess).reshape(LAST_ROWS // 8, 8, scen), axis=0)

    passes = line_dev // LAST_ROWS
    share = lax.fori_loop(0, passes, last_pass, jnp.zeros((8, scen), jnp.float32))
    share = jnp.sum(share, axis=0, keepdims=True)

    if small:
        shares[here] = share

        def pen_copy(step):
            other = lax.rem(here + step, areas)
            return pltpu.make_async_remote_copy(
                src_ref=shares.at[here],
                dst_ref=shares.at[here],
                send_sem=pen_send.at[other],
                recv_sem=pen_recv.at[here],
                device_id={"lines": other},
                device_id_type=MESH,
            )

        def pen_wait(step):
            other = lax.rem(here + step, areas)
            return pltpu.make_async_remote_copy(
                src_ref=shares.at[other],
                dst_ref=shares.at[other],
                send_sem=pen_send.at[other],
                recv_sem=pen_recv.at[other],
                device_id={"lines": other},
                device_id_type=MESH,
            )

        for step in range(1, areas):
            pen_copy(step).start()
        to_core(chip).wait_send()
        to_y(chip).wait_send()

        @pl.when(z < 3)
        def _():
            up.wait_send()

        @pl.when(z > 0)
        def _():
            down.wait_send()

        for i in range(4):
            to_core(across + 2 * steps[i]).wait_send()
        for i in range(1, 4):
            of = chip + 2 * steps[i]
            back = z - signs[i]

            @pl.when((back >= 0) & (back <= 3))
            def _():
                to_z(of, -signs[i]).wait_send()

            to_y(of).wait_send()

            @pl.when(steps[i] * signs[i] != 2)
            def _():
                to_core(of).wait_send()

        for i in range(passes):
            post_out(i).wait()
        for step in range(1, areas):
            pen_wait(step).wait_recv()
        total = shares[0]
        for area in range(1, areas):
            total = total + shares[area]
        pen_ref[...] = total / (line_dev * areas)
        for step in range(1, areas):
            pen_copy(step).wait_send()
    else:
        to_core(chip).wait_send()
        for step in away:
            direct(step).wait_send()
            to_core(lax.rem(chip + step + chips, chips)).wait_send()
        for i in range(passes):
            post_out(i).wait()
        pen_ref[...] = share


def on_device(base_flow, lodf_blocks, block_row, block_col, block_count, outage, rating, cost):
    areas = lax.axis_size("lines")
    nb, blk, _ = lodf_blocks.shape
    line_dev, scen = base_flow.shape
    rows_blocks = line_dev // blk
    near = 2 * NEAR + 1
    small = areas == 16
    slots = near + 1
    vmem = pl.BlockSpec(memory_space=pltpu.VMEM)
    smem = pl.BlockSpec(memory_space=pltpu.SMEM)
    anywhere = pl.BlockSpec(memory_space=pl.ANY)
    dma = pltpu.SemaphoreType.DMA
    post, pen = pl.pallas_call(
        functools.partial(kernel, areas),
        out_shape=(
            jax.ShapeDtypeStruct((line_dev, scen), jnp.bfloat16),
            jax.ShapeDtypeStruct((1, scen), jnp.float32),
        ),
        in_specs=[anywhere, anywhere, vmem, vmem, smem, vmem, vmem, vmem],
        out_specs=(anywhere, vmem),
        scratch_shapes=[
            pltpu.VMEM((line_dev, scen), jnp.bfloat16),
            pltpu.VMEM((nb + 1, blk, blk), jnp.bfloat16),
            pltpu.VMEM((near, line_dev, 2 * blk), jnp.bfloat16),
            pltpu.VMEM((rows_blocks * 2 * near, 128), jnp.int32),
            pltpu.SMEM((rows_blocks * 2 * near, 128), jnp.int32),
            pltpu.VMEM((slots, 2, blk, scen), jnp.bfloat16),
            pltpu.VMEM((line_dev, scen), jnp.float32),
            pltpu.VMEM((line_dev, scen), jnp.bfloat16),
            pltpu.VMEM((line_dev, blk), jnp.float32),
            pltpu.VMEM((line_dev, blk), jnp.float32),
            pltpu.VMEM((areas, 1, scen), jnp.float32),
            dma((2,)),
            dma((line_dev // LAST_ROWS,)),
            dma,
            dma((slots, 2)),
            dma((slots,)),
            dma((slots,)),
            dma((slots,)),
            dma((slots,)),
            dma((areas,)),
            dma((areas,)),
        ],
        compiler_params=pltpu.CompilerParams(
            collective_id=0, has_side_effects=True, vmem_limit_bytes=50 * 1024 * 1024
        ),
        cost_estimate=pl.CostEstimate(
            flops=2 * line_dev * 2 * near * blk * scen, bytes_accessed=11000000, transcendentals=0
        ),
    )(
        base_flow,
        lodf_blocks,
        block_row.reshape(1, nb),
        block_col.reshape(1, nb),
        block_count,
        outage.reshape(1, blk),
        rating.reshape(rows_blocks, blk),
        cost.reshape(rows_blocks, blk),
    )
    pen = pen.reshape(scen)
    if not small:
        pen = lax.psum(pen, "lines") / (line_dev * areas)
    return post, pen


def solution(mesh):
    return jax.shard_map(
        on_device,
        mesh=mesh,
        in_specs=(
            P("lines", "groups"),
            P("lines", None, None),
            P("lines"),
            P("lines"),
            P("lines"),
            P("lines"),
            P("lines"),
            P("lines"),
        ),
        out_specs=(P("lines", "groups"), P("groups")),
        check_vma=False,
    )
```

time: 202 us -> 42.2 us (0.21)
  matrix products: 87 us -> 0 us
  Pallas kernels: 0 us -> 35.3 us
  blocking collectives: 34 us -> 0 us
  waiting for transfers between devices: 27.9 us -> 0 us
  local copies, waits for them, and re-layouts: 27.3 us -> 5.3 us
  starting transfers between devices: 14.4 us -> 0 us
  other arithmetic: 9.72 us -> 0 us
    dot_general x12 -> x0, matrix products: 87 us -> none  [the longest x6 64.1 us: add_group(): jnp.einsum('rg,gis->ris', picker, terms, precision=lax.Precision.HIGHEST)]
    pallas_call x0 -> x1, Pallas kernels: none -> 35.3 us  [on_device(): pl.pallas_call(functools.partial(kernel, areas), out_shape=(jax.ShapeDtyp...]
    psum x1 -> x0, blocking collectives: 34 us -> none  [on_device(): total = lax.psum(share, 'lines')]
    ppermute x12 -> x0, waiting for transfers between devices: 27.9 us -> none  [passed_along(): lax.ppermute(array, axis, [(i, (i + by) % length) for i in range(length)])]
    gather x7 -> x0, local copies, waits for them, and re-layouts: 19.5 us -> none  [the longest x6 16.7 us: fetch(): return jnp.take(table, offset, axis=0)]
    ppermute x12 -> x0, starting transfers between devices: 14.4 us -> none  [passed_along(): lax.ppermute(array, axis, [(i, (i + by) % length) for i in range(length)])]
    unnamed x19 -> x12, local copies, waits for them, and re-layouts: 0.13 us -> 5.3 us
    and x7 -> x0, other arithmetic: 5.06 us -> none  [the longest x6 4.4 us: fetch(): return jnp.take(table, offset, axis=0)]
  transfers between devices with their start and end apart: 12 -> 0, of which waited for: 8 -> 0; matrix products, arithmetic and copies ran while one was open for 0% -> 0% of each run, Pallas kernels for 0% -> 0%
where the time goes in v1:
time: 42.2 us; the launch traced here: 41.9 us
  Pallas kernels  35.3 us (84%)
  local copies, waits for them, and re-layouts  5.3 us (13%)
  between operations  1.3 us (3%)
    pallas_call x1, Pallas kernels, on_device(): pl.pallas_call(functools.partial(kernel, areas), out_shape=(jax.ShapeDtyp...  35.3 us
    unnamed x12, local copies, waits for them, and re-layouts  5.3 us

profile of v1, /device:TPU:0, one launch (start us, length us, event | category | flops | bytes accessed | tf_op | source)
XLA Modules:
  0.0 41.9 jit_solution(3347259508548942686)
XLA Ops:
  1.3 0.0 copy-start
  1.3 0.7 %copy-done = s32[2048]{0:T(1024)S(1)} copy-done((s32[2048]{0:T(1024)S(1)}, s32[2048]{0:T(1024)}, u32[]{:S(2)}) %copy-start) | copy-done | bytes 8216
  2.0 0.0 copy-start.1
  2.0 0.7 %copy-done.1 = f32[2048]{0:T(1024)S(1)} copy-done((f32[2048]{0:T(1024)S(1)}, f32[2048]{0:T(1024)}, u32[]{:S(2)}) %copy-start.1) | copy-done | bytes 8216
  2.7 0.0 copy-start.2
  2.7 0.7 %copy-done.2 = s32[192]{0:T(256)S(1)} copy-done((s32[192]{0:T(256)S(1)}, s32[192]{0:T(256)}, u32[]{:S(2)}) %copy-start.2) | copy-done | bytes 792
  3.4 0.0 copy-start.3
  3.4 0.7 %copy-done.3 = s32[192]{0:T(256)S(1)} copy-done((s32[192]{0:T(256)S(1)}, s32[192]{0:T(256)}, u32[]{:S(2)}) %copy-start.3) | copy-done | bytes 792
  4.0 0.0 copy-start.4
  4.0 0.7 %copy-done.4 = s32[128]{0:T(128)S(1)} copy-done((s32[128]{0:T(128)S(1)}, s32[128]{0:T(128)}, u32[]{:S(2)}) %copy-start.4) | copy-done | bytes 536
  4.7 35.3 %shard_map.95 = (bf16[2048,512]{1,0:T(8,128)(2,1)S(1)}, f32[1,512]{1,0:T(1,128)S(1)}) custom-call(bf16[2048,512]{1,0:T(8,128)(2,1)} %base_hbm.1, bf16[192,128,128]{2,1,0:T(8,128)(2,1)} %lodf_hbm.1, s32[1,192]{1,0:T(1,128)S(1)} %bitcast.9, s32[1,192]{1,0:T(1,128)S(1)} %bitcast.10, s32[1]{0:T(128)S(6)} %copy.12.count_ref, s32[1,128]{1,0:T(1,128)S(1)} %bitcast.11, ...), custom_call_target="tpu_custom_call" | custom-call | flops 3758096384 | bytes 11000000 | tf_op jit(solution)/shard_map/pallas_call | solution.py:323
  40.0 1.3 %copy.13 = bf16[2048,512]{1,0:T(8,128)(2,1)} copy(bf16[2048,512]{1,0:T(8,128)(2,1)S(1)} %get-tuple-element.8) | data formatting | bytes 4194304
  41.3 0.6 %copy.14 = f32[512]{0:T(512)} copy(f32[512]{0:T(512)S(1)} %bitcast.6) | data formatting | bytes 4096
Async XLA Ops:
  1.3 0.7 %copy-start = (s32[2048]{0:T(1024)S(1)}, s32[2048]{0:T(1024)}, u32[]{:S(2)}) copy-start(s32[2048]{0:T(1024)} %param.14) | copy-start | bytes 24580
  2.0 0.7 %copy-start.1 = (f32[2048]{0:T(1024)S(1)}, f32[2048]{0:T(1024)}, u32[]{:S(2)}) copy-start(f32[2048]{0:T(1024)} %param.15) | copy-start | bytes 24580
  2.7 0.7 %copy-start.2 = (s32[192]{0:T(256)S(1)}, s32[192]{0:T(256)}, u32[]{:S(2)}) copy-start(s32[192]{0:T(256)} %param.10) | copy-start | bytes 2308
  3.4 0.7 %copy-start.3 = (s32[192]{0:T(256)S(1)}, s32[192]{0:T(256)}, u32[]{:S(2)}) copy-start(s32[192]{0:T(256)} %param.11) | copy-start | bytes 2308
  4.0 0.7 %copy-start.4 = (s32[128]{0:T(128)S(1)}, s32[128]{0:T(128)}, u32[]{:S(2)}) copy-start(s32[128]{0:T(128)} %param.13) | copy-start | bytes 1540

commit v2 on v1

--- a/solution.py
+++ b/solution.py
@@ -14,8 +14,8 @@
 LAST_ROWS = 256
 
 
-def kernel(areas, base_hbm, lodf_hbm, row_ref, col_ref, count_ref, outage_ref, rating_ref, cost_ref,
-           post_hbm, pen_ref, base, lodf, table, inv_v, inv_s, panels, acc, post, limit, weight,
+def kernel(areas, base_hbm, lodf_hbm, row_hbm, col_hbm, count_hbm, outage_hbm, rating_hbm, cost_hbm,
+           post_hbm, pen_ref, row_ref, col_ref, count_ref, outage_ref, rating_ref, cost_ref, base, lodf, table, inv_v, inv_s, panels, acc, post, limit, weight,
            shares, in_sem, out_sem, inv_sem, z_send, y_send, core_send, off_recv, core_recv,
            pen_send, pen_recv):
     chips = areas // 2
@@ -31,7 +31,17 @@
     partner = chip * 2 + 1 - core
 
     base_in = pltpu.make_async_copy(base_hbm, base, in_sem.at[0])
+    small_in = [
+        pltpu.make_async_copy(there, own, in_sem.at[2 + i])
+        for i, (there, own) in enumerate([
+            (outage_hbm, outage_ref), (row_hbm, row_ref), (col_hbm, col_ref),
+            (count_hbm, count_ref), (rating_hbm, rating_ref), (cost_hbm, cost_ref),
+        ])
+    ]
+    small_in[0].start()
     base_in.start()
+    for copy in small_in[1:]:
+        copy.start()
     lodf_in = pltpu.make_async_copy(lodf_hbm, lodf.at[pl.ds(0, nb)], in_sem.at[1])
     lodf_in.start()
 
@@ -64,6 +74,7 @@
     def off_wait(of):
         remote(of, chip, core, y_send.at[0], off_recv).wait_recv()
 
+    small_in[0].wait()
     picked = jnp.transpose(jnp.broadcast_to(outage_ref[...].astype(jnp.float32), (blk, blk)))
     lane = lax.broadcasted_iota(jnp.int32, (blk, blk), 1)
     ones = jnp.concatenate(
@@ -74,7 +85,6 @@
     panels[NEAR, core] = jnp.dot(ones, base[...], preferred_element_type=jnp.float32).astype(jnp.bfloat16)
     pl.semaphore_wait(barrier, len(peers))
 
-    to_core(chip).start()
     if small:
         y = lax.rem(chip, 2)
         z = chip // 2
@@ -89,7 +99,6 @@
         def to_z(of, by):
             return remote(of, chip + 2 * by, core, z_send.at[slot(of, chip), (by + 1) // 2], off_recv)
 
-        to_y(chip).start()
         up, down = to_z(chip, 1), to_z(chip, -1)
 
         @pl.when(z < 3)
@@ -99,6 +108,8 @@
         @pl.when(z > 0)
         def _():
             down.start()
+
+        to_y(chip).start()
     else:
         away = [step for step in range(-NEAR, NEAR + 1) if step != 0]
 
@@ -108,7 +119,10 @@
 
         for step in away:
             direct(step).start()
-
+    to_core(chip).start()
+
+    for copy in small_in[1:]:
+        copy.wait()
     offset = lax.rem(col_ref[...] - (2 * chip - REACH) + 2 * areas, areas)
     number = lax.broadcasted_iota(jnp.int32, (1, nb), 1)
     code = jnp.where(number < count_ref[0], row_ref[...] * width + offset, -1)
@@ -317,7 +331,7 @@
     small = areas == 16
     slots = near + 1
     vmem = pl.BlockSpec(memory_space=pltpu.VMEM)
-    smem = pl.BlockSpec(memory_space=pltpu.SMEM)
+    in_hbm = pl.BlockSpec(memory_space=pltpu.HBM)
     anywhere = pl.BlockSpec(memory_space=pl.ANY)
     dma = pltpu.SemaphoreType.DMA
     post, pen = pl.pallas_call(
@@ -326,9 +340,15 @@
             jax.ShapeDtypeStruct((line_dev, scen), jnp.bfloat16),
             jax.ShapeDtypeStruct((1, scen), jnp.float32),
         ),
-        in_specs=[anywhere, anywhere, vmem, vmem, smem, vmem, vmem, vmem],
+        in_specs=[in_hbm] * 8,
         out_specs=(anywhere, vmem),
         scratch_shapes=[
+            pltpu.VMEM((1, nb), jnp.int32),
+            pltpu.VMEM((1, nb), jnp.int32),
+            pltpu.SMEM((1,), jnp.int32),
+            pltpu.VMEM((1, blk), jnp.int32),
+            pltpu.VMEM((rows_blocks, blk), jnp.int32),
+            pltpu.VMEM((rows_blocks, blk), jnp.float32),
             pltpu.VMEM((line_dev, scen), jnp.bfloat16),
             pltpu.VMEM((nb + 1, blk, blk), jnp.bfloat16),
             pltpu.VMEM((near, line_dev, 2 * blk), jnp.bfloat16),
@@ -340,7 +360,7 @@
             pltpu.VMEM((line_dev, blk), jnp.float32),
             pltpu.VMEM((line_dev, blk), jnp.float32),
             pltpu.VMEM((areas, 1, scen), jnp.float32),
-            dma((2,)),
+            dma((8,)),
             dma((line_dev // LAST_ROWS,)),
             dma,
             dma((slots, 2)),
@@ -352,7 +372,7 @@
             dma((areas,)),
         ],
         compiler_params=pltpu.CompilerParams(
-            collective_id=0, has_side_effects=True, vmem_limit_bytes=50 * 1024 * 1024
+            collective_id=0, has_side_effects=True, vmem_limit_bytes=63 * 1024 * 1024
         ),
         cost_estimate=pl.CostEstimate(
             flops=2 * line_dev * 2 * near * blk * scen, bytes_accessed=11000000, transcendentals=0

time: 42.2 us -> 40.6 us (0.962)
  local copies, waits for them, and re-layouts: 5.3 us -> 3.63 us
    unnamed x12 -> x4, local copies, waits for them, and re-layouts: 5.3 us -> 3.63 us
where the time goes in v2:
time: 40.6 us; the launch traced here: 40.5 us
  Pallas kernels  35.5 us (87%)
  local copies, waits for them, and re-layouts  3.63 us (9%)
  between operations  1.29 us (3%)
    pallas_call x1, Pallas kernels, on_device(): pl.pallas_call(functools.partial(kernel, areas), out_shape=(jax.ShapeDtyp...  35.5 us
    unnamed x4, local copies, waits for them, and re-layouts  3.63 us

profile of v2, /device:TPU:0, one launch (start us, length us, event | category | flops | bytes accessed | tf_op | source)
XLA Modules:
  0.0 40.5 jit_solution(5027545968210240947)
XLA Ops:
  1.3 35.5 %shard_map.95 = (bf16[2048,512]{1,0:T(8,128)(2,1)}, f32[1,512]{1,0:T(1,128)}) custom-call(bf16[2048,512]{1,0:T(8,128)(2,1)} %base_hbm.1, bf16[192,128,128]{2,1,0:T(8,128)(2,1)} %lodf_hbm.1, s32[1,192]{1,0:T(1,128)} %bitcast.9, s32[1,192]{1,0:T(1,128)} %bitcast.10, s32[1]{0:T(128)S(6)} %copy.12.count_hbm, s32[1,128]{1,0:T(1,128)} %bitcast.11, ...), custom_call_target="tpu_custom_call" | custom-call | flops 3758096384 | bytes 11000000 | tf_op jit(solution)/shard_map/pallas_call | solution.py:337
  36.8 0.0 copy-start
  36.8 3.0 %copy.13 = bf16[2048,512]{1,0:T(8,128)(2,1)} copy(bf16[2048,512]{1,0:T(8,128)(2,1)} %get-tuple-element.8) | data formatting | bytes 4194304
  39.9 0.0 copy-done
  39.9 0.6 %copy.14 = f32[512]{0:T(512)} copy(f32[512]{0:T(512)S(1)} %bitcast.6) | data formatting | bytes 4096
Async XLA Ops:
  36.8 3.1 %copy-start = (f32[1,512]{1,0:T(1,128)S(1)}, f32[1,512]{1,0:T(1,128)}, u32[]{:S(2)}) copy-start(f32[1,512]{1,0:T(1,128)} %get-tuple-element.5) | copy-start | bytes 6148
